TPU v7x, 128 devices: a whole 4x4x4 slice. The times are simulated.
128 devices in a mesh: section: 2 (over core), expert: 16 (over z, y), head: 4 (over x).
Axes of the slice: x: 4, y: 4, z: 4, core: 2. Of those that a mesh axis runs over, the one named last changes fastest.
Arguments:
- inputs: bfloat16 [2, 2048, 768], P(None, 'expert'), may hold values from -6 to 6
- cotangent: bfloat16 [2, 2048, 768], P(None, 'expert'), may hold values from -6 to 6
- routes: int32 [2, 2, 2048, 2], P('section', None, 'expert'), may hold values from 0 to 31, all different within a row; in each aligned block of 128 rows (0 to 127, 128 to 255, ..., all dimensions but the last counted through in order) at most 12 rows name the same one
- attend_gain: bfloat16 [2, 768], P('section'), may hold values from 0.099609375 to 1.8984375
- query_key_value: bfloat16 [2, 3, 768, 768], P('section', None, None, 'head'), may hold values from -0.21875 to 0.21875
- attend_out: bfloat16 [2, 768, 768], P('section', 'head'), may hold values from -1.75 to 1.75
- position_bias: bfloat16 [2, 12, 32], P('section', 'head'), may hold values from -4 to 4
- mixture_gain: bfloat16 [2, 768], P('section'), may hold values from 0.099609375 to 1.8984375
- router: bfloat16 [2, 768, 32], P('section'), may hold values from -0.15625 to 0.15625
- expert_up: bfloat16 [2, 32, 768, 3072], P('section', 'expert', None, 'head'), may hold values from -0.21875 to 0.21875
- expert_down: bfloat16 [2, 32, 3072, 768], P('section', 'expert', 'head'), may hold values from -0.109375 to 0.109375
Outputs:
- section_output: bfloat16 [2, 2, 2048, 768], P('section', None, 'expert')
- input_grad: float32 [2, 2, 2048, 768], P('section', None, 'expert')
- grad_attend_gain: float32 [2, 768], P('section')
- grad_query_key_value: float32 [2, 3, 768, 768], P('section', None, None, 'head')
- grad_attend_out: float32 [2, 768, 768], P('section', 'head')
- grad_position_bias: float32 [2, 12, 32], P('section', 'head')
- grad_mixture_gain: float32 [2, 768], P('section')
- grad_router: float32 [2, 768, 32], P('section')
- grad_expert_up: float32 [2, 32, 768, 3072], P('section', 'expert', None, 'head')
- grad_expert_down: float32 [2, 32, 3072, 768], P('section', 'expert', 'head')
Inputs may be any that keep to these rules, and one draw needn't show every extreme that they name: `routes`: each token names two different experts. Among the 128 tokens of one sequence (one section, micro-batch and index of expert), no expert is named more than 12 times over both slots, and in every draw some expert is named exactly 12 times by some sequence.
All inputs are finite; a program needn't handle non-finite values.
Results may differ from a plain program's by a relative error of at most 0.028.
Values may be sent and summed in bfloat16 or wider, within the bound.
No kernel may reach another device: no remote copies, remote signals or barrier semaphores. Data moves between devices by JAX's collectives and lax.ppermute only.
A program may use at most 128 MiB of HBM per device.

v0:
```python
import jax
import jax.numpy as jnp
from jax import lax
from jax.sharding import PartitionSpec as P

HEAD_DIM = 64
EPS = 1e-06
NEG = -1e30


def passed_along(array, axis, by):
    length = lax.axis_size(axis)
    pairs = [(i, i + by) for i in range(length) if 0 <= i + by < length]
    return lax.ppermute(array, axis, pairs)


def norm_scale(values):
    return lax.rsqrt(jnp.mean(values * values, axis=-1, keepdims=True) + EPS)


def norm_back(grad_normed, values, scale, gain):
    unit = values * scale
    grad_gain = jnp.sum(grad_normed * unit, axis=0)
    grad_unit = grad_normed * gain
    grad_values = scale * (grad_unit - unit * jnp.mean(grad_unit * unit, axis=-1, keepdims=True))
    return (grad_values, grad_gain)


def position_tables(length, buckets):
    rows = lax.broadcasted_iota(jnp.int32, (length, length), 0)
    cols = lax.broadcasted_iota(jnp.int32, (length, length), 1)
    offset = rows - cols
    levels = lax.broadcasted_iota(jnp.int32, (buckets, length, length), 0)
    onehot = (jnp.clip(offset, 0, buckets - 1)[None] == levels).astype(jnp.bfloat16)
    return (offset >= 0, onehot)


def slot_targets(route_tile, experts, capacity):
    flat = route_tile.reshape(-1)
    levels = lax.broadcasted_iota(jnp.int32, (flat.shape[0], experts), 1)
    onehot = (flat[:, None] == levels).astype(jnp.int32)
    place = jnp.sum((jnp.cumsum(onehot, axis=0) - 1) * onehot, axis=1)
    return flat * capacity + place


def attend_scores(heads, table, causal, onehot):
    bias = jnp.einsum("bst,hb->hst", onehot, table, preferred_element_type=jnp.float32)
    scores = jnp.einsum("shd,thd->hst", heads[0], heads[1], preferred_element_type=jnp.float32)
    scores = scores * HEAD_DIM ** (-0.5) + bias
    return jnp.where(causal[None], scores, NEG)


def attend_forward(normed, proj_weight, out_weight, table, causal, onehot):
    length = normed.shape[0]
    local_heads = table.shape[0]
    projected = jnp.einsum(
        "sd,kde->kse", normed, proj_weight, preferred_element_type=jnp.float32
    ).astype(jnp.bfloat16)
    heads = projected.reshape(3, length, local_heads, HEAD_DIM)
    scores = attend_scores(heads, table, causal, onehot)
    top = jnp.max(scores, axis=-1, keepdims=True)
    weights = jnp.exp(scores - top)
    total = jnp.sum(weights, axis=-1, keepdims=True)
    probs = (weights / total).astype(jnp.bfloat16)
    mixed = jnp.einsum("hst,thd->shd", probs, heads[2], preferred_element_type=jnp.float32)
    mixed = mixed.reshape(length, local_heads * HEAD_DIM).astype(jnp.bfloat16)
    partial_out = jnp.dot(mixed, out_weight, preferred_element_type=jnp.float32)
    return (partial_out, (projected, mixed, top + jnp.log(total)))


def attend_backward(grad_attn, normed, proj_weight, out_weight, table, causal, onehot, saved_attn):
    projected, mixed, log_total = saved_attn
    length = normed.shape[0]
    local_heads = table.shape[0]
    heads = projected.reshape(3, length, local_heads, HEAD_DIM)
    grad_out_weight = jnp.einsum("se,sd->ed", mixed, grad_attn, preferred_element_type=jnp.float32)
    grad_mixed = jnp.einsum("sd,ed->se", grad_attn, out_weight, preferred_element_type=jnp.float32)
    grad_mixed = grad_mixed.astype(jnp.bfloat16).reshape(length, local_heads, HEAD_DIM)
    probs = jnp.exp(attend_scores(heads, table, causal, onehot) - log_total)
    grad_probs = jnp.einsum(
        "shd,thd->hst", grad_mixed, heads[2], preferred_element_type=jnp.float32
    )
    delta = jnp.sum(probs * grad_probs, axis=-1, keepdims=True)
    grad_scores = (probs * (grad_probs - delta)).astype(jnp.bfloat16)
    grad_table = jnp.einsum("bst,hst->hb", onehot, grad_scores, preferred_element_type=jnp.float32)
    factor = HEAD_DIM ** (-0.5)
    grad_query = (
        jnp.einsum("hst,thd->shd", grad_scores, heads[1], preferred_element_type=jnp.float32)
        * factor
    )
    grad_key = (
        jnp.einsum("hst,shd->thd", grad_scores, heads[0], preferred_element_type=jnp.float32)
        * factor
    )
    grad_value = jnp.einsum(
        "hst,shd->thd", probs.astype(jnp.bfloat16), grad_mixed, preferred_element_type=jnp.float32
    )
    grad_projected = (
        jnp.stack([grad_query, grad_key, grad_value])
        .reshape(3, length, local_heads * HEAD_DIM)
        .astype(jnp.bfloat16)
    )
    grad_proj_weight = jnp.einsum(
        "sd,kse->kde", normed, grad_projected, preferred_element_type=jnp.float32
    )
    grad_normed = jnp.einsum(
        "kse,kde->sd", grad_projected, proj_weight, preferred_element_type=jnp.float32
    )
    return (grad_normed, grad_proj_weight, grad_out_weight, grad_table)


def raise_hidden(arrived, up_weight):
    pre_act = jnp.einsum("erd,edf->erf", arrived, up_weight, preferred_element_type=jnp.float32)
    return (pre_act, jax.nn.gelu(pre_act).astype(jnp.bfloat16))


def gate_forward(logits, route_tile, experts):
    levels = lax.broadcasted_iota(jnp.int32, route_tile.shape + (experts,), 2)
    pick = (route_tile[:, :, None] == levels).astype(jnp.float32)
    chosen = jnp.sum(logits[:, None, :] * pick, axis=-1)
    top = jnp.max(chosen, axis=-1, keepdims=True)
    weights = jnp.exp(chosen - top)
    return (weights / jnp.sum(weights, axis=-1, keepdims=True), pick)


def layer_forward(layer_in, route_tile, params, tables):
    gain_a, proj_weight, out_weight, table, gain_m, router_weight, up_weight, down_weight = params
    causal, onehot = tables
    values = layer_in.astype(jnp.float32)
    length, width = values.shape
    experts = router_weight.shape[1]
    local_experts = up_weight.shape[0]
    capacity = 3 * length // experts
    scale_a = norm_scale(values)
    normed_a = (values * scale_a * gain_a).astype(jnp.bfloat16)
    partial_attn, saved_attn = attend_forward(
        normed_a, proj_weight, out_weight, table, causal, onehot
    )
    attended = lax.psum(partial_attn, "head")
    middle = values + attended
    scale_m = norm_scale(middle)
    normed_m = (middle * scale_m * gain_m).astype(jnp.bfloat16)
    logits = jnp.dot(normed_m, router_weight, preferred_element_type=jnp.float32)
    gates, pick = gate_forward(logits, route_tile, experts)
    target = slot_targets(route_tile, experts, capacity)
    buffer = (
        jnp.zeros((experts * capacity, width), jnp.bfloat16)
        .at[target]
        .set(jnp.repeat(normed_m, 2, axis=0))
    )
    arrived = lax.all_to_all(
        buffer.reshape(experts, 1, capacity, width),
        "expert",
        split_axis=0,
        concat_axis=1,
        tiled=True,
    )
    arrived = arrived.reshape(local_experts, -1, width)
    pre_act, hidden = raise_hidden(arrived, up_weight)
    partial_rows = jnp.einsum(
        "erf,efd->erd", hidden, down_weight, preferred_element_type=jnp.float32
    )
    returned = lax.all_to_all(
        partial_rows.reshape(local_experts, -1, capacity, width).astype(jnp.bfloat16),
        "expert",
        split_axis=1,
        concat_axis=0,
        tiled=True,
    ).astype(jnp.float32)
    slot_part = returned.reshape(experts * capacity, width)[target].reshape(length, 2, width)
    slot_out = lax.psum(slot_part.astype(jnp.bfloat16), "head").astype(jnp.float32)
    layer_out = middle + jnp.sum(gates[:, :, None] * slot_out, axis=1)
    owner_saved = (buffer,)
    saved = (
        values,
        scale_a,
        normed_a,
        saved_attn,
        middle,
        scale_m,
        normed_m,
        gates,
        pick,
        target,
        slot_out,
        owner_saved,
    )
    return (layer_out, saved)


def layer_backward(grad_out, saved, params, tables):
    gain_a, proj_weight, out_weight, table, gain_m, router_weight, up_weight, down_weight = params
    causal, onehot = tables
    (
        values,
        scale_a,
        normed_a,
        saved_attn,
        middle,
        scale_m,
        normed_m,
        gates,
        pick,
        target,
        slot_out,
        owner_saved,
    ) = saved
    length, width = values.shape
    experts = router_weight.shape[1]
    local_experts = up_weight.shape[0]
    capacity = 3 * length // experts
    grad_slots = (gates[:, :, None] * grad_out[:, None, :]).astype(jnp.bfloat16)
    grad_gates = jnp.sum(grad_out[:, None, :] * slot_out, axis=-1)
    grad_buffer = (
        jnp.zeros((experts * capacity, width), jnp.bfloat16)
        .at[target]
        .set(grad_slots.reshape(2 * length, width))
    )
    grad_buffer = grad_buffer.reshape(experts, 1, capacity, width)
    row_buffer = owner_saved[0].reshape(experts, 1, capacity, width)
    grad_arrived, arrived = (
        lax.all_to_all(grad_buffer, "expert", split_axis=0, concat_axis=1, tiled=True),
        lax.all_to_all(row_buffer, "expert", split_axis=0, concat_axis=1, tiled=True),
    )
    arrived = arrived.reshape(local_experts, -1, width)
    pre_act, hidden = raise_hidden(arrived, up_weight)
    grad_arrived = grad_arrived.reshape(local_experts, -1, width)
    grad_hidden = jnp.einsum(
        "erd,efd->erf", grad_arrived, down_weight, preferred_element_type=jnp.float32
    )
    unused, gelu_back = jax.vjp(jax.nn.gelu, pre_act)
    grad_pre = gelu_back(grad_hidden)[0].astype(jnp.bfloat16)
    grad_down = jnp.einsum("erf,erd->efd", hidden, grad_arrived, preferred_element_type=jnp.float32)
    grad_up = jnp.einsum("erd,erf->edf", arrived, grad_pre, preferred_element_type=jnp.float32)
    grad_rows = jnp.einsum("erf,edf->erd", grad_pre, up_weight, preferred_element_type=jnp.float32)
    returned = lax.all_to_all(
        grad_rows.reshape(local_experts, -1, capacity, width).astype(jnp.bfloat16),
        "expert",
        split_axis=1,
        concat_axis=0,
        tiled=True,
    ).astype(jnp.float32)
    grad_slot_rows = returned.reshape(experts * capacity, width)[target].reshape(length, 2, width)
    grad_normed_m = lax.psum(jnp.sum(grad_slot_rows, axis=1).astype(jnp.bfloat16), "head").astype(
        jnp.float32
    )
    grad_chosen = gates * (grad_gates - jnp.sum(gates * grad_gates, axis=-1, keepdims=True))
    grad_logits = jnp.sum(grad_chosen[:, :, None] * pick, axis=1).astype(jnp.bfloat16)
    grad_router = jnp.einsum("sd,se->de", normed_m, grad_logits, preferred_element_type=jnp.float32)
    grad_normed_m = grad_normed_m + jnp.einsum(
        "se,de->sd", grad_logits, router_weight, preferred_element_type=jnp.float32
    )
    grad_middle, grad_gain_m = norm_back(grad_normed_m, middle, scale_m, gain_m)
    grad_middle = grad_middle + grad_out
    grad_normed_a, grad_proj_weight, grad_out_weight, grad_table = attend_backward(
        grad_middle.astype(jnp.bfloat16),
        normed_a,
        proj_weight,
        out_weight,
        table,
        causal,
        onehot,
        saved_attn,
    )
    grad_normed_a = lax.psum(grad_normed_a.astype(jnp.bfloat16), "head").astype(jnp.float32)
    grad_values, grad_gain_a = norm_back(grad_normed_a, values, scale_a, gain_a)
    shared = (grad_gain_a, grad_proj_weight, grad_out_weight, grad_table, grad_gain_m, grad_router)
    return (grad_values + grad_middle, shared, (grad_up, grad_down))


def on_device(
    inputs,
    cotangent,
    routes,
    attend_gain,
    query_key_value,
    attend_out,
    position_bias,
    mixture_gain,
    router,
    expert_up,
    expert_down,
):
    micro = inputs.shape[0]
    length = inputs.shape[1]
    params = (
        attend_gain[0].astype(jnp.float32),
        query_key_value[0],
        attend_out[0],
        position_bias[0],
        mixture_gain[0].astype(jnp.float32),
        router[0],
        expert_up[0],
        expert_down[0],
    )
    tables = position_tables(length, position_bias.shape[2])
    first = lax.axis_index("section") == 0
    received = jnp.zeros((length, inputs.shape[2]), jnp.bfloat16)
    outputs = []
    caches = []
    for tick in range(micro + 1):
        layer_in = jnp.where(first, inputs[min(tick, micro - 1)], received)
        route_tile = jnp.where(first, routes[0, min(tick, micro - 1)], routes[0, max(tick - 1, 0)])
        layer_out, saved = layer_forward(layer_in, route_tile, params, tables)
        layer_low = layer_out.astype(jnp.bfloat16)
        outputs.append(layer_low)
        caches.append(saved)
        if tick < micro:
            received = passed_along(layer_low, "section", 1)
    section_output = jnp.stack(
        [jnp.where(first, outputs[index], outputs[index + 1]) for index in range(micro)]
    )[None]
    grad_received = jnp.zeros_like(received)
    shared_total = None
    owned_total = None
    grad_list = []
    for tick in range(micro + 1):
        late = cotangent[min(tick, micro - 1)].astype(jnp.float32)
        if tick == micro:
            late = jnp.zeros_like(late)
        grad_out = jnp.where(first, grad_received.astype(jnp.float32), late)
        saved = jax.tree.map(
            lambda early, later: jnp.where(first, early, later),
            caches[max(tick - 1, 0)],
            caches[min(tick + 1, micro)],
        )
        grad_in, shared, owned = layer_backward(grad_out, saved, params, tables)
        if shared_total is None:
            shared_total = shared
            owned_total = owned
        else:
            shared_total = jax.tree.map(lambda total, extra: total + extra, shared_total, shared)
            owned_total = jax.tree.map(lambda total, extra: total + extra, owned_total, owned)
        grad_list.append(grad_in)
        if tick < micro:
            grad_received = passed_along(grad_in.astype(jnp.bfloat16), "section", -1)
    gain_a, proj_part, out_part, table_part, gain_m, router_part = shared_total
    shared_total = (
        lax.psum(gain_a.astype(jnp.bfloat16), "expert").astype(jnp.float32),
        lax.psum(proj_part.astype(jnp.bfloat16), "expert").astype(jnp.float32),
        lax.psum(out_part.astype(jnp.bfloat16), "expert").astype(jnp.float32),
        lax.psum(table_part.astype(jnp.bfloat16), "expert").astype(jnp.float32),
        lax.psum(gain_m.astype(jnp.bfloat16), "expert").astype(jnp.float32),
        lax.psum(router_part.astype(jnp.bfloat16), "expert").astype(jnp.float32),
    )
    input_grad = jnp.stack(
        [jnp.where(first, grad_list[index + 1], grad_list[index]) for index in range(micro)]
    )[None]
    grad_gain_a, grad_proj, grad_out_weight, grad_table, grad_gain_m, grad_router = shared_total
    grad_up, grad_down = owned_total
    return (
        section_output,
        input_grad,
        grad_gain_a[None],
        grad_proj[None],
        grad_out_weight[None],
        grad_table[None],
        grad_gain_m[None],
        grad_router[None],
        grad_up[None],
        grad_down[None],
    )


def solution(mesh):
    return jax.shard_map(
        on_device,
        mesh=mesh,
        in_specs=(
            P(None, "expert", None),
            P(None, "expert", None),
            P("section", None, "expert", None),
            P("section", None),
            P("section", None, None, "head"),
            P("section", "head", None),
            P("section", "head", None),
            P("section", None),
            P("section", None, None),
            P("section", "expert", None, "head"),
            P("section", "expert", "head", None),
        ),
        out_specs=(
            P("section", None, "expert", None),
            P("section", None, "expert", None),
            P("section", None),
            P("section", None, None, "head"),
            P("section", "head", None),
            P("section", "head", None),
            P("section", None),
            P("section", None, None),
            P("section", "expert", None, "head"),
            P("section", "expert", "head", None),
        ),
        check_vma=False,
    )
```

profile of v0, /device:TPU:0, one launch (start us, length us, event | category | flops | bytes accessed | tf_op | source)
XLA Modules:
  0.0 950.1 jit_solution(12501314368429168360)
XLA Ops:
  22.1 39.1 %all-reduce.16.cloned.1.call-done = f32[128,768]{1,0:T(8,128)} async-done(((f32[128,768]{1,0:T(8,128)}), f32[128,768]{1,0:T(8,128)}) %all-reduce.16.cloned.1.call-update) | async-done | bytes 393232 | tf_op jit(solution)/shard_map/psum | solution.py:139
  68.0 19.2 %all_to_all.189 = bf16[32,1,12,768]{3,2,1,0:T(8,128)(2,1)S(1)} all-to-all(bf16[32,1,12,768]{3,2,1,0:T(8,128)(2,1)} %bitcast.600), channel_id=1, replica_groups=mesh['section'=2,'expert'=16,'head'=4] {'expert'}, dimensions={0} | all-to-all | bytes 1179648 | tf_op jit(solution)/shard_map/all_to_all | solution.py:151
  88.1 3.7 fusion.44
  91.9 2.5 copy.237
  94.4 3.6 all-to-all-start.1
  98.2 10.2 %all-to-all-done.1 = bf16[2,16,12,768]{3,0,2,1:T(2,128)(2,1)S(1)} async-done(((bf16[2,16,12,768]{3,0,2,1:T(2,128)(2,1)}), bf16[2,16,12,768]{3,0,2,1:T(2,128)(2,1)S(1)}, u32[]{:S(2)}, u32[]{:S(2)}) %all-to-all-start.1) | async-done | bytes 589856 | tf_op jit(solution)/shard_map/all_to_all | solution.py:163
  114.5 38.0 %all-reduce.18.cloned.1.call-done = bf16[128,2,768]{2,1,0:T(2,128)(2,1)} async-done(((bf16[128,2,768]{2,1,0:T(2,128)(2,1)}), bf16[128,2,768]{2,1,0:T(2,128)(2,1)}) %all-reduce.18.cloned.1.call-update) | async-done | bytes 393232 | tf_op jit(solution)/shard_map/psum | solution.py:171
  164.4 40.4 %all-reduce.20.cloned.1.call-done = f32[128,768]{1,0:T(8,128)} async-done(((f32[128,768]{1,0:T(8,128)}), f32[128,768]{1,0:T(8,128)}) %all-reduce.20.cloned.1.call-update) | async-done | bytes 393232 | tf_op jit(solution)/shard_map/psum | solution.py:139
  214.6 7.0 all-to-all-start.7
  225.1 8.9 all-to-all-done.7
  234.0 4.3 all-to-all-start.2
  239.5 2.7 scatter_custom_fusion.3
  244.1 5.9 all-to-all-done.2
  250.1 4.3 all-to-all-start.6
  259.3 3.8 fusion.47
  263.1 2.5 copy.249
  266.0 6.9 all-to-all-start.3
  281.0 2.4 all-to-all-done.3
  284.2 5.0 all-to-all-start.8
  304.9 2.5 reshape.1260
  307.4 2.9 reduce_sum.462
  310.8 3.0 fusion.217
  313.8 3.1 fusion.176
  317.0 37.1 %all-reduce.36.cloned.1.call-done = (bf16[128,768]{1,0:T(8,128)(2,1)}, bf16[128,2,768]{2,1,0:T(2,128)(2,1)}) async-done(((bf16[128,768]{1,0:T(8,128)(2,1)}, bf16[128,2,768]{2,1,0:T(2,128)(2,1)}), (bf16[128,768]{1,0:T(8,128)(2,1)}, bf16[128,2,768]{2,1,0:T(2,128)(2,1)})) %all-reduce.36.cloned.1.call-update) | async-done | bytes 589840 | tf_op jit(solution)/shard_map/psum | solution.py:244
  354.1 4.0 fusion.170
  369.2 38.2 %all-reduce.24.cloned.1.call-done = bf16[128,768]{1,0:T(8,128)(2,1)} async-done(((bf16[128,768]{1,0:T(8,128)(2,1)}), bf16[128,768]{1,0:T(8,128)(2,1)}) %all-reduce.24.cloned.1.call-update) | async-done | bytes 196624 | tf_op jit(solution)/shard_map/psum | solution.py:265
  418.4 2.6 fusion.291
  420.9 37.7 %all-reduce.22.cloned.1.call-done = f32[128,768]{1,0:T(8,128)} async-done(((f32[128,768]{1,0:T(8,128)}), f32[128,768]{1,0:T(8,128)}) %all-reduce.22.cloned.1.call-update) | async-done | bytes 393232 | tf_op jit(solution)/shard_map/psum | solution.py:139
  464.9 2.9 scatter_custom_fusion.2
  472.0 7.2 all-to-all-start.13
  486.3 5.2 all-to-all-done.13
  491.6 4.5 all-to-all-start.4
  504.0 6.3 all-to-all-done.4
  510.3 4.3 all-to-all-start.10
  515.2 2.7 scatter_custom_fusion.4
  520.0 7.7 all-to-all-done.10
  527.6 4.3 all-to-all-start.9
  538.2 2.9 fusion.50
  544.7 7.4 all-to-all-start.5
  560.1 2.5 all-to-all-done.5
  562.6 4.8 all-to-all-start.11
  567.5 3.0 fusion.212
  584.4 2.5 reshape.1266
  586.9 2.8 reduce_sum.469
  591.9 3.1 fusion.177
  595.1 37.2 %all-reduce.34.cloned.1.call-done = (bf16[128,768]{1,0:T(8,128)(2,1)}, bf16[128,2,768]{2,1,0:T(2,128)(2,1)}) async-done(((bf16[128,768]{1,0:T(8,128)(2,1)}, bf16[128,2,768]{2,1,0:T(2,128)(2,1)}), (bf16[128,768]{1,0:T(8,128)(2,1)}, bf16[128,2,768]{2,1,0:T(2,128)(2,1)})) %all-reduce.34.cloned.1.call-update) | async-done | bytes 589840 | tf_op jit(solution)/shard_map/psum | solution.py:244
  643.4 2.7 fusion.289
  646.2 2.4 convolution_add_fusion.1
  649.4 39.0 %all-reduce.26.cloned.1.call-done = bf16[128,768]{1,0:T(8,128)(2,1)} async-done(((bf16[128,768]{1,0:T(8,128)(2,1)}), bf16[128,768]{1,0:T(8,128)(2,1)}) %all-reduce.26.cloned.1.call-update) | async-done | bytes 196624 | tf_op jit(solution)/shard_map/psum | solution.py:265
  690.2 2.3 select_bitcast_fusion
  696.6 2.7 fusion.175
  702.5 2.7 scatter_custom_fusion.5
  707.3 7.2 all-to-all-start.12
  717.3 11.9 %all-to-all-done.12 = bf16[32,1,12,768]{3,2,1,0:T(8,128)(2,1)} async-done(((bf16[32,1,12,768]{3,2,1,0:T(8,128)(2,1)}), bf16[32,1,12,768]{3,2,1,0:T(8,128)(2,1)}, u32[]{:S(2)}, u32[]{:S(2)}) %all-to-all-start.12) | async-done | bytes 589856 | tf_op jit(solution)/shard_map/all_to_all | solution.py:222
  731.4 3.1 fusion.74
  736.9 4.2 all-to-all-start.14
  741.2 7.2 add_bitcast_fusion
  748.5 4.2 all-to-all-done.14
  762.5 7.3 add_bitcast_fusion.1
  769.7 30.9 %all-reduce.28.cloned.1.call-done = bf16[128,768]{1,0:T(8,128)(2,1)} async-done(((bf16[128,768]{1,0:T(8,128)(2,1)}), bf16[128,768]{1,0:T(8,128)(2,1)}) %all-reduce.28.cloned.1.call-update) | async-done | bytes 196624 | tf_op jit(solution)/shard_map/psum | solution.py:244
  806.6 3.5 fusion.34
  816.8 31.7 %all-reduce.30.cloned.1.call-done = bf16[128,768]{1,0:T(8,128)(2,1)} async-done(((bf16[128,768]{1,0:T(8,128)(2,1)}), bf16[128,768]{1,0:T(8,128)(2,1)}) %all-reduce.30.cloned.1.call-update) | async-done | bytes 196624 | tf_op jit(solution)/shard_map/psum | solution.py:265
  850.9 75.9 %all-reduce = (bf16[1,3,32]{2,1,0:T(4,128)(2,1)}, bf16[1,768]{1,0:T(2,128)(2,1)}, bf16[1,768]{1,0:T(2,128)(2,1)S(1)}, bf16[1,768,32]{1,2,0:T(8,128)(2,1)}) all-reduce(bf16[1,3,32]{2,1,0:T(4,128)(2,1)} %fusion.153, bf16[1,768]{1,0:T(2,128)(2,1)S(1)} %broadcast_in_dim.93, ...), channel_id=1, replica_groups=mesh['section'=2,'expert'=16,'head'=4] {'expert'}, use_global_device_ids=true, to_apply=%region_78.79 | all-reduce | flops 26208 | bytes 104832 | tf_op jit(solution)/shard_map/psum | solution.py:342
  934.2 6.0 all-reduce.32.cloned.1.call-done
  (761 shorter events, 235.5 us)
Async XLA Ops:
  7.2 80.9 %copy-start = (bf16[1,2,768,768]{3,2,1,0:T(8,128)(2,1)S(1)}, bf16[1,2,768,768]{3,2,1,0:T(8,128)(2,1)}, u32[]{:S(2)}) copy-start(bf16[1,2,768,768]{3,2,1,0:T(8,128)(2,1)} %param.20) | copy-start | bytes 7077892
  7.2 54.1 %all-reduce.16.cloned.1.call-start = ((), (), s32[]{:S(2)}) async-start(), calls=%async_computation.15 | async-start | bytes 786432 | tf_op jit(solution)/shard_map/psum | solution.py:139
  8.6 149.8 %copy-start.203 = (f32[128]{0:T(128)}, f32[128]{0:T(128)S(1)}, u32[]{:S(2)}) copy-start(f32[128]{0:T(128)S(1)} %fusion.245) | copy-start | bytes 1540
  9.3 149.7 %copy-start.103 = (f32[768]{0:T(1024)}, f32[768]{0:T(1024)S(1)}, u32[]{:S(2)}) copy-start(f32[768]{0:T(1024)S(1)} %convert_reduce_fusion.1) | copy-start | bytes 9220
  15.5 45.8 %copy-start.14 = (bf16[2,128,768]{2,1,0:T(8,128)(2,1)S(1)}, bf16[2,128,768]{2,1,0:T(8,128)(2,1)}, u32[]{:S(2)}) copy-start(bf16[2,128,768]{2,1,0:T(8,128)(2,1)} %param.11) | copy-start | bytes 1179652
  17.1 96.1 %copy-start.171 = (s32[128,2]{0,1:T(2,128)}, s32[128,2]{0,1:T(2,128)S(1)}, u32[]{:S(2)}) copy-start(s32[128,2]{0,1:T(2,128)S(1)} %get-tuple-element.130) | copy-start | bytes 3076
  20.6 185.8 %copy-start.119 = (f32[768]{0:T(1024)}, f32[768]{0:T(1024)S(1)}, u32[]{:S(2)}) copy-start(f32[768]{0:T(1024)S(1)} %convert_reduce_fusion) | copy-start | bytes 9220
  62.4 143.5 %copy-start.205 = (f32[128]{0:T(128)}, f32[128]{0:T(128)S(1)}, u32[]{:S(2)}) copy-start(f32[128]{0:T(128)S(1)} %multiply_reduce_fusion.8) | copy-start | bytes 1540
  94.4 14.0 %all-to-all-start.1 = ((bf16[2,16,12,768]{3,0,2,1:T(2,128)(2,1)}), bf16[2,16,12,768]{3,0,2,1:T(2,128)(2,1)S(1)}, u32[]{:S(2)}, u32[]{:S(2)}) async-start(bf16[2,16,12,768]{3,0,2,1:T(2,128)(2,1)} %bitcast.613), calls=%async_computation.1 | async-start | bytes 1179648 | tf_op jit(solution)/shard_map/all_to_all | solution.py:163
  97.9 54.5 %all-reduce.18.cloned.1.call-start = ((), (), s32[]{:S(2)}) async-start(), calls=%async_computation.16 | async-start | bytes 786432 | tf_op jit(solution)/shard_map/psum | solution.py:171
  113.2 91.6 %all-reduce.20.cloned.1.call-start = ((), (), s32[]{:S(2)}) async-start(), calls=%async_computation.17 | async-start | bytes 786432 | tf_op jit(solution)/shard_map/psum | solution.py:139
  114.5 44.6 %copy-start.9 = (bf16[1,3,768,192]{2,3,1,0:T(8,128)(2,1)S(1)}, bf16[1,3,768,192]{2,3,1,0:T(8,128)(2,1)}, u32[]{:S(2)}) copy-start(bf16[1,3,768,192]{2,3,1,0:T(8,128)(2,1)} %param.15) | copy-start | bytes 2654212
  155.7 2.5 collective-permute-start
  158.4 48.0 %copy-start.1 = (bf16[128,768]{1,0:T(8,128)(2,1)}, bf16[128,768]{1,0:T(8,128)(2,1)S(1)}, u32[]{:S(2)}) copy-start(bf16[128,768]{1,0:T(8,128)(2,1)S(1)} %get-tuple-element.96) | copy-start | bytes 589828
  214.6 19.4 %all-to-all-start.7 = ((bf16[32,1,12,768]{3,2,1,0:T(8,128)(2,1)}), bf16[32,1,12,768]{3,2,1,0:T(8,128)(2,1)}, u32[]{:S(2)}, u32[]{:S(2)}) async-start(bf16[32,1,12,768]{3,2,1,0:T(8,128)(2,1)} %bitcast.598), calls=%async_computation.7 | async-start | bytes 1572864 | tf_op jit(solution)/shard_map/all_to_all | solution.py:223
  234.0 16.1 %all-to-all-start.2 = ((bf16[32,1,12,768]{3,2,1,0:T(8,128)(2,1)}), bf16[32,1,12,768]{3,2,1,0:T(8,128)(2,1)}, u32[]{:S(2)}, u32[]{:S(2)}) async-start(bf16[32,1,12,768]{3,2,1,0:T(8,128)(2,1)} %bitcast.596), calls=%async_computation.2 | async-start | bytes 1572864 | tf_op jit(solution)/shard_map/all_to_all | solution.py:151
  250.1 15.9 %all-to-all-start.6 = ((bf16[32,1,12,768]{3,2,1,0:T(8,128)(2,1)}), bf16[32,1,12,768]{3,2,1,0:T(8,128)(2,1)}, u32[]{:S(2)}, u32[]{:S(2)}) async-start(bf16[32,1,12,768]{3,2,1,0:T(8,128)(2,1)} %bitcast.80), calls=%async_computation.6 | async-start | bytes 1572864 | tf_op jit(solution)/shard_map/all_to_all | solution.py:222
  266.0 17.4 %all-to-all-start.3 = ((bf16[2,16,12,768]{3,0,2,1:T(2,128)(2,1)}), bf16[2,16,12,768]{3,0,2,1:T(2,128)(2,1)S(1)}, u32[]{:S(2)}, u32[]{:S(2)}) async-start(bf16[2,16,12,768]{3,0,2,1:T(2,128)(2,1)} %bitcast.611), calls=%async_computation.3 | async-start | bytes 1179648 | tf_op jit(solution)/shard_map/all_to_all | solution.py:163
  284.2 15.4 %all-to-all-start.8 = ((bf16[2,16,12,768]{3,0,2,1:T(2,128)(2,1)}), bf16[2,16,12,768]{3,0,2,1:T(2,128)(2,1)S(1)}, u32[]{:S(2)}, u32[]{:S(2)}) async-start(bf16[2,16,12,768]{3,0,2,1:T(2,128)(2,1)} %bitcast.88), calls=%async_computation.8 | async-start | bytes 1179648 | tf_op jit(solution)/shard_map/all_to_all | solution.py:236
  289.1 64.9 %all-reduce.36.cloned.1.call-start = ((), (), s32[]{:S(2)}) async-start(), calls=%async_computation.25 | async-start | bytes 1179648 | tf_op jit(solution)/shard_map/psum | solution.py:244
  310.3 97.2 %all-reduce.24.cloned.1.call-start = ((), (), s32[]{:S(2)}) async-start(), calls=%async_computation.19 | async-start | bytes 393216 | tf_op jit(solution)/shard_map/psum | solution.py:265
  313.8 40.3 %copy-start.127 = (f32[128,2]{1,0:T(8,128)S(1)}, f32[128,2]{1,0:T(8,128)}, u32[]{:S(2)}) copy-start(f32[128,2]{1,0:T(8,128)} %copy.240) | copy-start | bytes 3076
  316.9 42.1 %copy-start.167 = (f32[128,2]{0,1:T(2,128)S(1)}, f32[128,2]{0,1:T(2,128)}, u32[]{:S(2)}) copy-start(f32[128,2]{0,1:T(2,128)} %copy-done.166) | copy-start | bytes 3076
  316.9 42.2 %copy-start.172 = (s32[128,2]{0,1:T(2,128)S(1)}, s32[128,2]{0,1:T(2,128)}, u32[]{:S(2)}) copy-start(s32[128,2]{0,1:T(2,128)} %copy-done.171) | copy-start | bytes 3076
  316.9 42.2 %copy-start.175 = (s32[128,2]{0,1:T(2,128)S(1)}, s32[128,2]{0,1:T(2,128)}, u32[]{:S(2)}) copy-start(s32[128,2]{0,1:T(2,128)} %broadcast_select_fusion.26) | copy-start | bytes 3076
  316.9 42.8 %copy-start.2 = (bf16[128,768]{1,0:T(8,128)(2,1)S(1)}, bf16[128,768]{1,0:T(8,128)(2,1)}, u32[]{:S(2)}) copy-start(bf16[128,768]{1,0:T(8,128)(2,1)} %copy-done.1) | copy-start | bytes 589828
  316.9 42.8 %copy-start.16 = (bf16[2,128,768]{2,1,0:T(8,128)(2,1)S(1)}, bf16[2,128,768]{2,1,0:T(8,128)(2,1)}, u32[]{:S(2)}) copy-start(bf16[2,128,768]{2,1,0:T(8,128)(2,1)} %param.11) | copy-start | bytes 1179652
  316.9 42.8 %copy-start.24 = (f32[128,768]{1,0:T(8,128)S(1)}, f32[128,768]{1,0:T(8,128)}, u32[]{:S(2)}) copy-start(f32[128,768]{1,0:T(8,128)} %all-reduce.16.cloned.1.call-done) | copy-start | bytes 1179652
  316.9 42.8 %copy-start.82 = (bf16[1,768,32]{1,2,0:T(8,128)(2,1)S(1)}, bf16[1,768,32]{1,2,0:T(8,128)(2,1)}, u32[]{:S(2)}) copy-start(bf16[1,768,32]{1,2,0:T(8,128)(2,1)} %param.19) | copy-start | bytes 147460
  316.9 42.8 %copy-start.120 = (f32[768]{0:T(1024)S(1)}, f32[768]{0:T(1024)}, u32[]{:S(2)}) copy-start(f32[768]{0:T(1024)} %copy-done.119) | copy-start | bytes 9220
  316.9 42.8 %copy-start.201 = (f32[128]{0:T(128)S(1)}, f32[128]{0:T(128)}, u32[]{:S(2)}) copy-start(f32[128]{0:T(128)} %get-tuple-element.144) | copy-start | bytes 1540
  365.2 93.4 %all-reduce.22.cloned.1.call-start = ((), (), s32[]{:S(2)}) async-start(), calls=%async_computation.18 | async-start | bytes 786432 | tf_op jit(solution)/shard_map/psum | solution.py:139
  367.3 42.1 %copy-start.98 = (bf16[128,768]{1,0:T(8,128)(2,1)}, bf16[128,768]{1,0:T(8,128)(2,1)S(1)}, u32[]{:S(2)}) copy-start(bf16[128,768]{1,0:T(8,128)(2,1)S(1)} %get-tuple-element.84) | copy-start | bytes 589828
  367.3 42.1 %collective-permute-start.1 = (bf16[128,768]{1,0:T(8,128)(2,1)S(1)}, bf16[128,768]{1,0:T(8,128)(2,1)}, u32[]{:S(2)}, u32[]{:S(2)}) collective-permute-start(bf16[128,768]{1,0:T(8,128)(2,1)S(1)} %get-tuple-element.84), channel_id=1, source_target_pairs={{0,64},{1,65},{2,66},{3,67},{4,68},{5,69},{6,70},{7,71},{8,72},{9,... | collective-permute-start | bytes 589832 | tf_op jit(solution)/shard_map/ppermute | solution.py:14
  411.4 48.9 %copy-start.5 = (bf16[128,768]{1,0:T(8,128)(2,1)}, bf16[128,768]{1,0:T(8,128)(2,1)S(1)}, u32[]{:S(2)}) copy-start(bf16[128,768]{1,0:T(8,128)(2,1)S(1)} %get-tuple-element.92) | copy-start | bytes 589828
  418.3 41.4 %copy-start.206 = (f32[128]{0:T(128)S(1)}, f32[128]{0:T(128)}, u32[]{:S(2)}) copy-start(f32[128]{0:T(128)} %copy-done.205) | copy-start | bytes 1540
  418.4 41.4 %copy-start.210 = (f32[128]{0:T(128)S(1)}, f32[128]{0:T(128)}, u32[]{:S(2)}) copy-start(f32[128]{0:T(128)} %copy-done.209) | copy-start | bytes 1540
  418.4 41.9 %copy-start.121 = (f32[768]{0:T(1024)S(1)}, f32[768]{0:T(1024)}, u32[]{:S(2)}) copy-start(f32[768]{0:T(1024)} %copy-done.119) | copy-start | bytes 9220
  472.0 19.5 %all-to-all-start.13 = ((bf16[32,1,12,768]{3,2,1,0:T(8,128)(2,1)}), bf16[32,1,12,768]{3,2,1,0:T(8,128)(2,1)}, u32[]{:S(2)}, u32[]{:S(2)}) async-start(bf16[32,1,12,768]{3,2,1,0:T(8,128)(2,1)} %bitcast.129), calls=%async_computation.13 | async-start | bytes 1572864 | tf_op jit(solution)/shard_map/all_to_all | solution.py:223
  481.3 16.1 %collective-permute-start.2 = (bf16[128,768]{1,0:T(8,128)(2,1)}, bf16[128,768]{1,0:T(8,128)(2,1)}, u32[]{:S(2)}, u32[]{:S(2)}) collective-permute-start(bf16[128,768]{1,0:T(8,128)(2,1)} %get-tuple-element.99), channel_id=1, source_target_pairs={{64,0},{65,1},{66,2},{67,3},{68,4},{69,5},{70,6},{71,7},{72,8},{73... | collective-permute-start | bytes 589832 | tf_op jit(solution)/shard_map/ppermute | solution.py:14
  491.6 18.7 %all-to-all-start.4 = ((bf16[32,1,12,768]{3,2,1,0:T(8,128)(2,1)}), bf16[32,1,12,768]{3,2,1,0:T(8,128)(2,1)}, u32[]{:S(2)}, u32[]{:S(2)}) async-start(bf16[32,1,12,768]{3,2,1,0:T(8,128)(2,1)} %bitcast.595), calls=%async_computation.4 | async-start | bytes 1572864 | tf_op jit(solution)/shard_map/all_to_all | solution.py:151
  510.3 17.3 %all-to-all-start.10 = ((bf16[32,1,12,768]{3,2,1,0:T(8,128)(2,1)}), bf16[32,1,12,768]{3,2,1,0:T(8,128)(2,1)}, u32[]{:S(2)}, u32[]{:S(2)}) async-start(bf16[32,1,12,768]{3,2,1,0:T(8,128)(2,1)} %bitcast.594), calls=%async_computation.10 | async-start | bytes 1572864 | tf_op jit(solution)/shard_map/all_to_all | solution.py:223
  527.6 17.1 %all-to-all-start.9 = ((bf16[32,1,12,768]{3,2,1,0:T(8,128)(2,1)}), bf16[32,1,12,768]{3,2,1,0:T(8,128)(2,1)}, u32[]{:S(2)}, u32[]{:S(2)}) async-start(bf16[32,1,12,768]{3,2,1,0:T(8,128)(2,1)} %bitcast.101), calls=%async_computation.9 | async-start | bytes 1572864 | tf_op jit(solution)/shard_map/all_to_all | solution.py:222
  544.7 17.9 %all-to-all-start.5 = ((bf16[2,16,12,768]{3,0,2,1:T(2,128)(2,1)}), bf16[2,16,12,768]{3,0,2,1:T(2,128)(2,1)}, u32[]{:S(2)}, u32[]{:S(2)}) async-start(bf16[2,16,12,768]{3,0,2,1:T(2,128)(2,1)} %bitcast.68), calls=%async_computation.5 | async-start | bytes 1179648 | tf_op jit(solution)/shard_map/all_to_all | solution.py:163
  562.6 15.4 %all-to-all-start.11 = ((bf16[2,16,12,768]{3,0,2,1:T(2,128)(2,1)}), bf16[2,16,12,768]{3,0,2,1:T(2,128)(2,1)}, u32[]{:S(2)}, u32[]{:S(2)}) async-start(bf16[2,16,12,768]{3,0,2,1:T(2,128)(2,1)} %bitcast.610), calls=%async_computation.11 | async-start | bytes 1179648 | tf_op jit(solution)/shard_map/all_to_all | solution.py:236
  567.4 64.8 %all-reduce.34.cloned.1.call-start = ((), (), s32[]{:S(2)}) async-start(), calls=%async_computation.24 | async-start | bytes 1179648 | tf_op jit(solution)/shard_map/psum | solution.py:244
  589.7 98.6 %all-reduce.26.cloned.1.call-start = ((), (), s32[]{:S(2)}) async-start(), calls=%async_computation.20 | async-start | bytes 393216 | tf_op jit(solution)/shard_map/psum | solution.py:265
  595.0 39.3 %copy-start.173 = (s32[128,2]{0,1:T(2,128)S(1)}, s32[128,2]{0,1:T(2,128)}, u32[]{:S(2)}) copy-start(s32[128,2]{0,1:T(2,128)} %copy-done.171) | copy-start | bytes 3076
  595.0 39.3 %copy-start.6 = (bf16[128,768]{1,0:T(8,128)(2,1)S(1)}, bf16[128,768]{1,0:T(8,128)(2,1)}, u32[]{:S(2)}) copy-start(bf16[128,768]{1,0:T(8,128)(2,1)} %copy-done.5) | copy-start | bytes 589828
  595.1 39.3 %copy-start.17 = (bf16[2,128,768]{2,1,0:T(8,128)(2,1)S(1)}, bf16[2,128,768]{2,1,0:T(8,128)(2,1)}, u32[]{:S(2)}) copy-start(bf16[2,128,768]{2,1,0:T(8,128)(2,1)} %param.11) | copy-start | bytes 1179652
  595.1 39.3 %copy-start.25 = (f32[128,768]{1,0:T(8,128)S(1)}, f32[128,768]{1,0:T(8,128)}, u32[]{:S(2)}) copy-start(f32[128,768]{1,0:T(8,128)} %all-reduce.16.cloned.1.call-done) | copy-start | bytes 1179652
  595.1 39.3 %copy-start.84 = (bf16[1,768,32]{1,2,0:T(8,128)(2,1)S(1)}, bf16[1,768,32]{1,2,0:T(8,128)(2,1)}, u32[]{:S(2)}) copy-start(bf16[1,768,32]{1,2,0:T(8,128)(2,1)} %param.19) | copy-start | bytes 147460
  595.1 39.3 %copy-start.122 = (f32[768]{0:T(1024)S(1)}, f32[768]{0:T(1024)}, u32[]{:S(2)}) copy-start(f32[768]{0:T(1024)} %copy-done.119) | copy-start | bytes 9220
  595.1 39.3 %copy-start.200 = (f32[128]{0:T(128)S(1)}, f32[128]{0:T(128)}, u32[]{:S(2)}) copy-start(f32[128]{0:T(128)} %get-tuple-element.141) | copy-start | bytes 1540
  646.1 42.3 %copy-start.18 = (bf16[2,128,768]{2,1,0:T(8,128)(2,1)S(1)}, bf16[2,128,768]{2,1,0:T(8,128)(2,1)}, u32[]{:S(2)}) copy-start(bf16[2,128,768]{2,1,0:T(8,128)(2,1)} %param.11) | copy-start | bytes 1179652
  646.1 44.0 %copy-start.3 = (bf16[128,768]{1,0:T(8,128)(2,1)S(1)}, bf16[128,768]{1,0:T(8,128)(2,1)}, u32[]{:S(2)}) copy-start(bf16[128,768]{1,0:T(8,128)(2,1)} %copy-done.1) | copy-start | bytes 589828
  646.2 44.0 %copy-start.31 = (f32[128,768]{1,0:T(8,128)S(1)}, f32[128,768]{1,0:T(8,128)}, u32[]{:S(2)}) copy-start(f32[128,768]{1,0:T(8,128)} %copy-done.29) | copy-start | bytes 1179652
  693.2 3.3 collective-permute-start.3
  707.3 22.0 %all-to-all-start.12 = ((bf16[32,1,12,768]{3,2,1,0:T(8,128)(2,1)}), bf16[32,1,12,768]{3,2,1,0:T(8,128)(2,1)}, u32[]{:S(2)}, u32[]{:S(2)}) async-start(bf16[32,1,12,768]{3,2,1,0:T(8,128)(2,1)} %bitcast.597), calls=%async_computation.12 | async-start | bytes 1572864 | tf_op jit(solution)/shard_map/all_to_all | solution.py:222
  736.9 15.8 %all-to-all-start.14 = ((bf16[2,16,12,768]{3,0,2,1:T(2,128)(2,1)}), bf16[2,16,12,768]{3,0,2,1:T(2,128)(2,1)}, u32[]{:S(2)}, u32[]{:S(2)}) async-start(bf16[2,16,12,768]{3,0,2,1:T(2,128)(2,1)} %bitcast.612), calls=%async_computation.14 | async-start | bytes 1179648 | tf_op jit(solution)/shard_map/all_to_all | solution.py:236
  741.2 59.4 %all-reduce.28.cloned.1.call-start = ((), (), s32[]{:S(2)}) async-start(), calls=%async_computation.21 | async-start | bytes 393216 | tf_op jit(solution)/shard_map/psum | solution.py:244
  762.4 86.1 %all-reduce.30.cloned.1.call-start = ((), (), s32[]{:S(2)}) async-start(), calls=%async_computation.22 | async-start | bytes 393216 | tf_op jit(solution)/shard_map/psum | solution.py:265
  806.5 133.6 %all-reduce.32.cloned.1.call-start = ((), (), s32[]{:S(2)}) async-start(), calls=%async_computation.23 | async-start | bytes 2359296 | tf_op jit(solution)/shard_map/psum | solution.py:340
  811.1 121.0 %copy-start.65 = (f32[128,768]{1,0:T(8,128)S(1)}, f32[128,768]{1,0:T(8,128)}, u32[]{:S(2)}) copy-start(f32[128,768]{1,0:T(8,128)} %copy-done.64) | copy-start | bytes 1179652
  (188 other events, 1151.2 us)
Sparse Core Ops, SparseCore 0:
  16.6 44.6 all-reduce.15
  113.3 39.0 all-reduce.17
  162.0 42.7 all-reduce.19
  310.4 43.6 all-reduce.35
  365.3 42.0 all-reduce.23
  415.9 42.6 all-reduce.21
  589.8 42.4 all-reduce.33
  646.2 42.0 all-reduce.25
  762.5 38.0 all-reduce.27
  806.6 41.8 all-reduce.29
  852.5 87.6 all-reduce.31
where the time goes:
time: 963 us; the launch traced here: 950 us
  waiting for transfers between devices  445 us (46%)
  local copies, waits for them, and re-layouts  132 us (14%)
  matrix products  95.4 us (10%)
  blocking collectives  95.1 us (10%)
  other arithmetic  83 us (9%)
  starting transfers between devices  82.3 us (9%)
  between operations  17 us (2%)
    psum x3, waiting for transfers between devices, layer_forward(): attended = lax.psum(partial_attn, 'head')  117 us
    psum x3, waiting for transfers between devices, layer_backward(): lax.psum(grad_normed_a.astype(jnp.bfloat16), 'head').astype(jnp.float32)  109 us
    psum x3, waiting for transfers between devices, layer_backward(): lax.psum(jnp.sum(grad_slot_rows, axis=1).astype(jnp.bfloat16), 'head')  105 us
    psum x1, blocking collectives, on_device(): lax.psum(table_part.astype(jnp.bfloat16), 'expert').astype(jnp.float32)  75.9 us
    psum x1, waiting for transfers between devices, layer_forward(): lax.psum(slot_part.astype(jnp.bfloat16), 'head').astype(jnp.float32)  38 us
    all_to_all x3, waiting for transfers between devices, layer_backward(): lax.all_to_all(row_buffer, 'expert', split_axis=0, concat_axis=1, tiled=T...  21.8 us
  transfers between devices with their start and end apart: 29, of which 26 were waited for; matrix products, arithmetic and copies ran while one was open for 16% of the time, Pallas kernels for 0%

commit v1 on v0

--- a/solution.py
+++ b/solution.py
@@ -262,7 +262,9 @@
         onehot,
         saved_attn,
     )
-    grad_normed_a = lax.psum(grad_normed_a.astype(jnp.bfloat16), "head").astype(jnp.float32)
+    grad_normed_a = jnp.sum(
+        lax.all_gather(grad_normed_a.astype(jnp.bfloat16), "head"), axis=0
+    ).astype(jnp.float32)
     grad_values, grad_gain_a = norm_back(grad_normed_a, values, scale_a, gain_a)
     shared = (grad_gain_a, grad_proj_weight, grad_out_weight, grad_table, grad_gain_m, grad_router)
     return (grad_values + grad_middle, shared, (grad_up, grad_down))

time: 963 us -> 888 us (0.922)
  waiting for transfers between devices: 445 us -> 332 us
  blocking collectives: 95.1 us -> 140 us
    psum x3 -> x0, waiting for transfers between devices: 109 us -> none  [layer_backward(): lax.psum(grad_normed_a.astype(jnp.bfloat16), 'head').astype(jnp.float32)]
    all_gather x0 -> x3, blocking collectives: none -> 45.1 us  [layer_backward(): lax.all_gather(grad_normed_a.astype(jnp.bfloat16), 'head')]
  transfers between devices with their start and end apart: 29 -> 26, of which waited for: 26 -> 21; matrix products, arithmetic and copies ran while one was open for 16% -> 16% of each run, Pallas kernels for 0% -> 0%
where the time goes in v1:
time: 888 us; the launch traced here: 876 us
  waiting for transfers between devices  332 us (37%)
  blocking collectives  140 us (16%)
  local copies, waits for them, and re-layouts  130 us (15%)
  matrix products  88.9 us (10%)
  other arithmetic  84.8 us (10%)
  starting transfers between devices  82.1 us (9%)
  between operations  17.5 us (2%)
    psum x3, waiting for transfers between devices, layer_forward(): attended = lax.psum(partial_attn, 'head')  116 us
    psum x3, waiting for transfers between devices, layer_backward(): lax.psum(jnp.sum(grad_slot_rows, axis=1).astype(jnp.bfloat16), 'head')  105 us
    psum x1, blocking collectives, on_device(): lax.psum(table_part.astype(jnp.bfloat16), 'expert').astype(jnp.float32)  76 us
    all_gather x3, blocking collectives, layer_backward(): lax.all_gather(grad_normed_a.astype(jnp.bfloat16), 'head')  45.1 us
    psum x1, waiting for transfers between devices, layer_forward(): lax.psum(slot_part.astype(jnp.bfloat16), 'head').astype(jnp.float32)  37.9 us
    all_to_all x3, waiting for transfers between devices, layer_backward(): lax.all_to_all(row_buffer, 'expert', split_axis=0, concat_axis=1, tiled=T...  21.8 us
    all_to_all x1, blocking collectives, layer_forward(): lax.all_to_all(buffer.reshape(experts, 1, capacity, width), 'expert', spl...  19.2 us
    all_to_all x3, starting transfers between devices, layer_backward(): lax.all_to_all(row_buffer, 'expert', split_axis=0, concat_axis=1, tiled=T...  18.5 us
  transfers between devices with their start and end apart: 26, of which 21 were waited for; matrix products, arithmetic and copies ran while one was open for 16% of the time, Pallas kernels for 0%

profile of v1, /device:TPU:0, one launch (start us, length us, event | category | flops | bytes accessed | tf_op | source)
XLA Modules:
  0.0 875.6 jit_solution(8453990208602040031)
XLA Ops:
  22.2 39.1 %all-reduce.13.cloned.1.call-done = f32[128,768]{1,0:T(8,128)} async-done(((f32[128,768]{1,0:T(8,128)}), f32[128,768]{1,0:T(8,128)}) %all-reduce.13.cloned.1.call-update) | async-done | bytes 393232 | tf_op jit(solution)/shard_map/psum | solution.py:139
  64.7 2.3 scatter_custom_fusion
  68.0 19.2 %all_to_all.189 = bf16[32,1,12,768]{3,2,1,0:T(8,128)(2,1)S(1)} all-to-all(bf16[32,1,12,768]{3,2,1,0:T(8,128)(2,1)} %bitcast.606), channel_id=1, replica_groups=mesh['section'=2,'expert'=16,'head'=4] {'expert'}, dimensions={0} | all-to-all | bytes 1179648 | tf_op jit(solution)/shard_map/all_to_all | solution.py:151
  88.1 3.8 fusion.44
  91.9 2.5 copy.237
  94.4 3.6 all-to-all-start.1
  98.2 10.2 %all-to-all-done.1 = bf16[2,16,12,768]{3,0,2,1:T(2,128)(2,1)S(1)} async-done(((bf16[2,16,12,768]{3,0,2,1:T(2,128)(2,1)}), bf16[2,16,12,768]{3,0,2,1:T(2,128)(2,1)S(1)}, u32[]{:S(2)}, u32[]{:S(2)}) %all-to-all-start.1) | async-done | bytes 589856 | tf_op jit(solution)/shard_map/all_to_all | solution.py:163
  114.6 37.9 %all-reduce.15.cloned.1.call-done = bf16[128,2,768]{2,1,0:T(2,128)(2,1)} async-done(((bf16[128,2,768]{2,1,0:T(2,128)(2,1)}), bf16[128,2,768]{2,1,0:T(2,128)(2,1)}) %all-reduce.15.cloned.1.call-update) | async-done | bytes 393232 | tf_op jit(solution)/shard_map/psum | solution.py:171
  152.5 2.1 fusion.167
  164.2 40.4 %all-reduce.17.cloned.1.call-done = f32[128,768]{1,0:T(8,128)} async-done(((f32[128,768]{1,0:T(8,128)}), f32[128,768]{1,0:T(8,128)}) %all-reduce.17.cloned.1.call-update) | async-done | bytes 393232 | tf_op jit(solution)/shard_map/psum | solution.py:139
  209.3 2.3 scatter_custom_fusion.1
  214.6 7.0 all-to-all-start.7
  225.0 8.9 %all-to-all-done.7 = bf16[32,1,12,768]{3,2,1,0:T(8,128)(2,1)} async-done(((bf16[32,1,12,768]{3,2,1,0:T(8,128)(2,1)}), bf16[32,1,12,768]{3,2,1,0:T(8,128)(2,1)}, u32[]{:S(2)}, u32[]{:S(2)}) %all-to-all-start.7) | async-done | bytes 589856 | tf_op jit(solution)/shard_map/all_to_all | solution.py:223
  233.9 4.3 all-to-all-start.2
  239.4 2.7 scatter_custom_fusion.3
  244.1 5.9 all-to-all-done.2
  250.0 4.3 all-to-all-start.6
  259.2 3.8 fusion.47
  263.0 2.5 copy.249
  265.9 6.9 all-to-all-start.3
  280.9 2.4 all-to-all-done.3
  284.1 4.9 all-to-all-start.8
  304.8 2.5 reshape.1260
  307.3 2.9 reduce_sum.498
  310.7 3.0 fusion.217
  313.8 3.1 fusion.176
  316.9 37.1 %all-reduce.27.cloned.1.call-done = (bf16[128,768]{1,0:T(8,128)(2,1)}, bf16[128,2,768]{2,1,0:T(2,128)(2,1)}) async-done(((bf16[128,768]{1,0:T(8,128)(2,1)}, bf16[128,2,768]{2,1,0:T(2,128)(2,1)}), (bf16[128,768]{1,0:T(8,128)(2,1)}, bf16[128,2,768]{2,1,0:T(2,128)(2,1)})) %all-reduce.27.cloned.1.call-update) | async-done | bytes 589840 | tf_op jit(solution)/shard_map/psum | solution.py:244
  354.0 4.0 fusion.170
  367.3 14.9 %all-gather = bf16[512,768]{1,0:T(8,128)(2,1)} all-gather(bf16[128,768]{1,0:T(8,128)(2,1)S(1)} %fusion.117), channel_id=2, replica_groups=mesh['section'=2,'expert'=16,'head'=4] {'head'}, dimensions={0}, use_global_device_ids=true | all-gather | bytes 983040 | tf_op jit(solution)/shard_map/all_gather | solution.py:266
  394.1 2.6 fusion.291
  396.7 37.0 %all-reduce.19.cloned.1.call-done = f32[128,768]{1,0:T(8,128)} async-done(((f32[128,768]{1,0:T(8,128)}), f32[128,768]{1,0:T(8,128)}) %all-reduce.19.cloned.1.call-update) | async-done | bytes 393232 | tf_op jit(solution)/shard_map/psum | solution.py:139
  440.0 2.9 scatter_custom_fusion.2
  442.9 2.2 broadcast_select_fusion
  447.1 7.2 all-to-all-start.13
  461.4 5.2 all-to-all-done.13
  466.6 4.5 all-to-all-start.4
  479.1 6.3 all-to-all-done.4
  485.4 4.3 all-to-all-start.10
  490.3 2.7 scatter_custom_fusion.4
  495.0 7.6 all-to-all-done.10
  502.6 4.3 all-to-all-start.9
  513.3 2.9 fusion.50
  519.7 7.2 all-to-all-start.5
  534.9 2.5 all-to-all-done.5
  537.4 4.7 all-to-all-start.11
  542.4 3.1 fusion.212
  559.0 2.5 reshape.1266
  561.5 2.8 reduce_sum.506
  566.1 3.1 fusion.177
  569.3 38.0 %all-reduce.25.cloned.1.call-done = (bf16[128,768]{1,0:T(8,128)(2,1)}, bf16[128,2,768]{2,1,0:T(2,128)(2,1)}) async-done(((bf16[128,768]{1,0:T(8,128)(2,1)}, bf16[128,2,768]{2,1,0:T(2,128)(2,1)}), (bf16[128,768]{1,0:T(8,128)(2,1)}, bf16[128,2,768]{2,1,0:T(2,128)(2,1)})) %all-reduce.25.cloned.1.call-update) | async-done | bytes 589840 | tf_op jit(solution)/shard_map/psum | solution.py:244
  620.4 15.2 %all-gather.1 = bf16[512,768]{1,0:T(8,128)(2,1)} all-gather(bf16[128,768]{1,0:T(8,128)(2,1)S(1)} %fusion.118), channel_id=3, replica_groups=mesh['section'=2,'expert'=16,'head'=4] {'head'}, dimensions={0}, use_global_device_ids=true | all-gather | bytes 983040 | tf_op jit(solution)/shard_map/all_gather | solution.py:266
  639.4 2.3 select_bitcast_fusion
  645.9 2.7 fusion.175
  651.7 2.7 scatter_custom_fusion.5
  656.5 7.0 all-to-all-start.12
  666.4 14.2 %all-to-all-done.12 = bf16[32,1,12,768]{3,2,1,0:T(8,128)(2,1)} async-done(((bf16[32,1,12,768]{3,2,1,0:T(8,128)(2,1)}), bf16[32,1,12,768]{3,2,1,0:T(8,128)(2,1)}, u32[]{:S(2)}, u32[]{:S(2)}) %all-to-all-start.12) | async-done | bytes 589856 | tf_op jit(solution)/shard_map/all_to_all | solution.py:222
  682.8 3.1 fusion.74
  688.3 4.3 all-to-all-start.14
  692.8 7.2 add_bitcast_fusion
  700.0 5.2 all-to-all-done.14
  715.0 7.2 add_bitcast_fusion.1
  722.2 30.2 %all-reduce.21.cloned.1.call-done = bf16[128,768]{1,0:T(8,128)(2,1)} async-done(((bf16[128,768]{1,0:T(8,128)(2,1)}), bf16[128,768]{1,0:T(8,128)(2,1)}) %all-reduce.21.cloned.1.call-update) | async-done | bytes 196624 | tf_op jit(solution)/shard_map/psum | solution.py:244
  757.2 15.1 %all-gather.2 = bf16[512,768]{1,0:T(8,128)(2,1)} all-gather(bf16[128,768]{1,0:T(8,128)(2,1)S(1)} %fusion.119), channel_id=4, replica_groups=mesh['section'=2,'expert'=16,'head'=4] {'head'}, dimensions={0}, use_global_device_ids=true | all-gather | bytes 983040 | tf_op jit(solution)/shard_map/all_gather | solution.py:266
  782.0 76.0 %all-reduce = (bf16[1,3,32]{2,1,0:T(4,128)(2,1)}, bf16[1,768]{1,0:T(2,128)(2,1)}, bf16[1,768]{1,0:T(2,128)(2,1)S(1)}, bf16[1,768,32]{1,2,0:T(8,128)(2,1)}) all-reduce(bf16[1,3,32]{2,1,0:T(4,128)(2,1)} %fusion.153, bf16[1,768]{1,0:T(2,128)(2,1)S(1)} %broadcast_in_dim.93, ...), channel_id=1, replica_groups=mesh['section'=2,'expert'=16,'head'=4] {'expert'}, use_global_device_ids=true, to_apply=%region_78.79 | all-reduce | flops 26208 | bytes 104832 | tf_op jit(solution)/shard_map/psum | solution.py:344
  (782 shorter events, 227.9 us)
Async XLA Ops:
  7.2 81.0 %copy-start = (bf16[1,2,768,768]{3,2,1,0:T(8,128)(2,1)S(1)}, bf16[1,2,768,768]{3,2,1,0:T(8,128)(2,1)}, u32[]{:S(2)}) copy-start(bf16[1,2,768,768]{3,2,1,0:T(8,128)(2,1)} %param.20) | copy-start | bytes 7077892
  7.2 54.1 %all-reduce.13.cloned.1.call-start = ((), (), s32[]{:S(2)}) async-start(), calls=%async_computation.15 | async-start | bytes 786432 | tf_op jit(solution)/shard_map/psum | solution.py:139
  8.6 149.8 %copy-start.215 = (f32[128]{0:T(128)}, f32[128]{0:T(128)S(1)}, u32[]{:S(2)}) copy-start(f32[128]{0:T(128)S(1)} %fusion.245) | copy-start | bytes 1540
  9.3 149.6 %copy-start.110 = (f32[768]{0:T(1024)}, f32[768]{0:T(1024)S(1)}, u32[]{:S(2)}) copy-start(f32[768]{0:T(1024)S(1)} %convert_reduce_fusion.1) | copy-start | bytes 9220
  15.5 45.8 %copy-start.14 = (bf16[2,128,768]{2,1,0:T(8,128)(2,1)S(1)}, bf16[2,128,768]{2,1,0:T(8,128)(2,1)}, u32[]{:S(2)}) copy-start(bf16[2,128,768]{2,1,0:T(8,128)(2,1)} %param.11) | copy-start | bytes 1179652
  17.1 96.2 %copy-start.183 = (s32[128,2]{0,1:T(2,128)}, s32[128,2]{0,1:T(2,128)S(1)}, u32[]{:S(2)}) copy-start(s32[128,2]{0,1:T(2,128)S(1)} %get-tuple-element.130) | copy-start | bytes 3076
  20.6 185.7 %copy-start.128 = (f32[768]{0:T(1024)}, f32[768]{0:T(1024)S(1)}, u32[]{:S(2)}) copy-start(f32[768]{0:T(1024)S(1)} %convert_reduce_fusion) | copy-start | bytes 9220
  62.4 143.3 %copy-start.217 = (f32[128]{0:T(128)}, f32[128]{0:T(128)S(1)}, u32[]{:S(2)}) copy-start(f32[128]{0:T(128)S(1)} %multiply_reduce_fusion.8) | copy-start | bytes 1540
  63.6 34.5 %copy-start.62 = (bf16[128,768]{1,0:T(8,128)(2,1)}, bf16[128,768]{1,0:T(8,128)(2,1)S(1)}, u32[]{:S(2)}) copy-start(bf16[128,768]{1,0:T(8,128)(2,1)S(1)} %multiply_convert_fusion.14) | copy-start | bytes 589828
  94.4 14.0 %all-to-all-start.1 = ((bf16[2,16,12,768]{3,0,2,1:T(2,128)(2,1)}), bf16[2,16,12,768]{3,0,2,1:T(2,128)(2,1)S(1)}, u32[]{:S(2)}, u32[]{:S(2)}) async-start(bf16[2,16,12,768]{3,0,2,1:T(2,128)(2,1)} %bitcast.619), calls=%async_computation.1 | async-start | bytes 1179648 | tf_op jit(solution)/shard_map/all_to_all | solution.py:163
  98.0 54.5 %all-reduce.15.cloned.1.call-start = ((), (), s32[]{:S(2)}) async-start(), calls=%async_computation.16 | async-start | bytes 786432 | tf_op jit(solution)/shard_map/psum | solution.py:171
  113.2 91.4 %all-reduce.17.cloned.1.call-start = ((), (), s32[]{:S(2)}) async-start(), calls=%async_computation.17 | async-start | bytes 786432 | tf_op jit(solution)/shard_map/psum | solution.py:139
  114.5 44.4 %copy-start.9 = (bf16[1,3,768,192]{2,3,1,0:T(8,128)(2,1)S(1)}, bf16[1,3,768,192]{2,3,1,0:T(8,128)(2,1)}, u32[]{:S(2)}) copy-start(bf16[1,3,768,192]{2,3,1,0:T(8,128)(2,1)} %param.15) | copy-start | bytes 2654212
  155.7 2.5 collective-permute-start
  158.4 48.0 %copy-start.1 = (bf16[128,768]{1,0:T(8,128)(2,1)}, bf16[128,768]{1,0:T(8,128)(2,1)S(1)}, u32[]{:S(2)}) copy-start(bf16[128,768]{1,0:T(8,128)(2,1)S(1)} %get-tuple-element.96) | copy-start | bytes 589828
  214.6 19.4 %all-to-all-start.7 = ((bf16[32,1,12,768]{3,2,1,0:T(8,128)(2,1)}), bf16[32,1,12,768]{3,2,1,0:T(8,128)(2,1)}, u32[]{:S(2)}, u32[]{:S(2)}) async-start(bf16[32,1,12,768]{3,2,1,0:T(8,128)(2,1)} %bitcast.602), calls=%async_computation.7 | async-start | bytes 1572864 | tf_op jit(solution)/shard_map/all_to_all | solution.py:223
  233.9 16.1 %all-to-all-start.2 = ((bf16[32,1,12,768]{3,2,1,0:T(8,128)(2,1)}), bf16[32,1,12,768]{3,2,1,0:T(8,128)(2,1)}, u32[]{:S(2)}, u32[]{:S(2)}) async-start(bf16[32,1,12,768]{3,2,1,0:T(8,128)(2,1)} %bitcast.600), calls=%async_computation.2 | async-start | bytes 1572864 | tf_op jit(solution)/shard_map/all_to_all | solution.py:151
  250.0 15.9 %all-to-all-start.6 = ((bf16[32,1,12,768]{3,2,1,0:T(8,128)(2,1)}), bf16[32,1,12,768]{3,2,1,0:T(8,128)(2,1)}, u32[]{:S(2)}, u32[]{:S(2)}) async-start(bf16[32,1,12,768]{3,2,1,0:T(8,128)(2,1)} %bitcast.80), calls=%async_computation.6 | async-start | bytes 1572864 | tf_op jit(solution)/shard_map/all_to_all | solution.py:222
  265.9 17.4 %all-to-all-start.3 = ((bf16[2,16,12,768]{3,0,2,1:T(2,128)(2,1)}), bf16[2,16,12,768]{3,0,2,1:T(2,128)(2,1)S(1)}, u32[]{:S(2)}, u32[]{:S(2)}) async-start(bf16[2,16,12,768]{3,0,2,1:T(2,128)(2,1)} %bitcast.617), calls=%async_computation.3 | async-start | bytes 1179648 | tf_op jit(solution)/shard_map/all_to_all | solution.py:163
  284.1 15.4 %all-to-all-start.8 = ((bf16[2,16,12,768]{3,0,2,1:T(2,128)(2,1)}), bf16[2,16,12,768]{3,0,2,1:T(2,128)(2,1)S(1)}, u32[]{:S(2)}, u32[]{:S(2)}) async-start(bf16[2,16,12,768]{3,0,2,1:T(2,128)(2,1)} %bitcast.88), calls=%async_computation.8 | async-start | bytes 1179648 | tf_op jit(solution)/shard_map/all_to_all | solution.py:236
  289.1 64.9 %all-reduce.27.cloned.1.call-start = ((), (), s32[]{:S(2)}) async-start(), calls=%async_computation.22 | async-start | bytes 1179648 | tf_op jit(solution)/shard_map/psum | solution.py:244
  310.2 123.4 %all-reduce.19.cloned.1.call-start = ((), (), s32[]{:S(2)}) async-start(), calls=%async_computation.18 | async-start | bytes 786432 | tf_op jit(solution)/shard_map/psum | solution.py:139
  313.8 40.2 %copy-start.136 = (f32[128,2]{1,0:T(8,128)S(1)}, f32[128,2]{1,0:T(8,128)}, u32[]{:S(2)}) copy-start(f32[128,2]{1,0:T(8,128)} %copy.240) | copy-start | bytes 3076
  316.8 42.1 %copy-start.179 = (f32[128,2]{0,1:T(2,128)S(1)}, f32[128,2]{0,1:T(2,128)}, u32[]{:S(2)}) copy-start(f32[128,2]{0,1:T(2,128)} %copy-done.178) | copy-start | bytes 3076
  316.8 42.1 %copy-start.184 = (s32[128,2]{0,1:T(2,128)S(1)}, s32[128,2]{0,1:T(2,128)}, u32[]{:S(2)}) copy-start(s32[128,2]{0,1:T(2,128)} %copy-done.183) | copy-start | bytes 3076
  316.8 42.1 %copy-start.187 = (s32[128,2]{0,1:T(2,128)S(1)}, s32[128,2]{0,1:T(2,128)}, u32[]{:S(2)}) copy-start(s32[128,2]{0,1:T(2,128)} %broadcast_select_fusion.26) | copy-start | bytes 3076
  316.8 42.8 %copy-start.2 = (bf16[128,768]{1,0:T(8,128)(2,1)S(1)}, bf16[128,768]{1,0:T(8,128)(2,1)}, u32[]{:S(2)}) copy-start(bf16[128,768]{1,0:T(8,128)(2,1)} %copy-done.1) | copy-start | bytes 589828
  316.8 42.8 %copy-start.16 = (bf16[2,128,768]{2,1,0:T(8,128)(2,1)S(1)}, bf16[2,128,768]{2,1,0:T(8,128)(2,1)}, u32[]{:S(2)}) copy-start(bf16[2,128,768]{2,1,0:T(8,128)(2,1)} %param.11) | copy-start | bytes 1179652
  316.9 42.8 %copy-start.25 = (f32[128,768]{1,0:T(8,128)S(1)}, f32[128,768]{1,0:T(8,128)}, u32[]{:S(2)}) copy-start(f32[128,768]{1,0:T(8,128)} %all-reduce.13.cloned.1.call-done) | copy-start | bytes 1179652
  316.9 42.7 %copy-start.89 = (bf16[1,768,32]{1,2,0:T(8,128)(2,1)S(1)}, bf16[1,768,32]{1,2,0:T(8,128)(2,1)}, u32[]{:S(2)}) copy-start(bf16[1,768,32]{1,2,0:T(8,128)(2,1)} %param.19) | copy-start | bytes 147460
  316.9 42.7 %copy-start.129 = (f32[768]{0:T(1024)S(1)}, f32[768]{0:T(1024)}, u32[]{:S(2)}) copy-start(f32[768]{0:T(1024)} %copy-done.128) | copy-start | bytes 9220
  316.9 42.7 %copy-start.213 = (f32[128]{0:T(128)S(1)}, f32[128]{0:T(128)}, u32[]{:S(2)}) copy-start(f32[128]{0:T(128)} %get-tuple-element.144) | copy-start | bytes 1540
  364.9 20.2 %collective-permute-start.1 = (bf16[128,768]{1,0:T(8,128)(2,1)}, bf16[128,768]{1,0:T(8,128)(2,1)}, u32[]{:S(2)}, u32[]{:S(2)}) collective-permute-start(bf16[128,768]{1,0:T(8,128)(2,1)} %get-tuple-element.84), channel_id=1, source_target_pairs={{0,64},{1,65},{2,66},{3,67},{4,68},{5,69},{6,70},{7,71},{8,72},{9,... | collective-permute-start | bytes 589832 | tf_op jit(solution)/shard_map/ppermute | solution.py:14
  387.1 48.2 %copy-start.5 = (bf16[128,768]{1,0:T(8,128)(2,1)}, bf16[128,768]{1,0:T(8,128)(2,1)S(1)}, u32[]{:S(2)}) copy-start(bf16[128,768]{1,0:T(8,128)(2,1)S(1)} %get-tuple-element.92) | copy-start | bytes 589828
  394.1 40.7 %copy-start.218 = (f32[128]{0:T(128)S(1)}, f32[128]{0:T(128)}, u32[]{:S(2)}) copy-start(f32[128]{0:T(128)} %copy-done.217) | copy-start | bytes 1540
  394.1 40.7 %copy-start.222 = (f32[128]{0:T(128)S(1)}, f32[128]{0:T(128)}, u32[]{:S(2)}) copy-start(f32[128]{0:T(128)} %copy-done.221) | copy-start | bytes 1540
  394.1 41.2 %copy-start.130 = (f32[768]{0:T(1024)S(1)}, f32[768]{0:T(1024)}, u32[]{:S(2)}) copy-start(f32[768]{0:T(1024)} %copy-done.128) | copy-start | bytes 9220
  447.1 19.5 %all-to-all-start.13 = ((bf16[32,1,12,768]{3,2,1,0:T(8,128)(2,1)}), bf16[32,1,12,768]{3,2,1,0:T(8,128)(2,1)}, u32[]{:S(2)}, u32[]{:S(2)}) async-start(bf16[32,1,12,768]{3,2,1,0:T(8,128)(2,1)} %bitcast.131), calls=%async_computation.13 | async-start | bytes 1572864 | tf_op jit(solution)/shard_map/all_to_all | solution.py:223
  456.3 16.1 %collective-permute-start.2 = (bf16[128,768]{1,0:T(8,128)(2,1)}, bf16[128,768]{1,0:T(8,128)(2,1)}, u32[]{:S(2)}, u32[]{:S(2)}) collective-permute-start(bf16[128,768]{1,0:T(8,128)(2,1)} %get-tuple-element.99), channel_id=1, source_target_pairs={{64,0},{65,1},{66,2},{67,3},{68,4},{69,5},{70,6},{71,7},{72,8},{73... | collective-permute-start | bytes 589832 | tf_op jit(solution)/shard_map/ppermute | solution.py:14
  466.6 18.7 %all-to-all-start.4 = ((bf16[32,1,12,768]{3,2,1,0:T(8,128)(2,1)}), bf16[32,1,12,768]{3,2,1,0:T(8,128)(2,1)}, u32[]{:S(2)}, u32[]{:S(2)}) async-start(bf16[32,1,12,768]{3,2,1,0:T(8,128)(2,1)} %bitcast.599), calls=%async_computation.4 | async-start | bytes 1572864 | tf_op jit(solution)/shard_map/all_to_all | solution.py:151
  485.4 17.3 %all-to-all-start.10 = ((bf16[32,1,12,768]{3,2,1,0:T(8,128)(2,1)}), bf16[32,1,12,768]{3,2,1,0:T(8,128)(2,1)}, u32[]{:S(2)}, u32[]{:S(2)}) async-start(bf16[32,1,12,768]{3,2,1,0:T(8,128)(2,1)} %bitcast.598), calls=%async_computation.10 | async-start | bytes 1572864 | tf_op jit(solution)/shard_map/all_to_all | solution.py:223
  502.6 17.1 %all-to-all-start.9 = ((bf16[32,1,12,768]{3,2,1,0:T(8,128)(2,1)}), bf16[32,1,12,768]{3,2,1,0:T(8,128)(2,1)}, u32[]{:S(2)}, u32[]{:S(2)}) async-start(bf16[32,1,12,768]{3,2,1,0:T(8,128)(2,1)} %bitcast.102), calls=%async_computation.9 | async-start | bytes 1572864 | tf_op jit(solution)/shard_map/all_to_all | solution.py:222
  519.7 17.7 %all-to-all-start.5 = ((bf16[2,16,12,768]{3,0,2,1:T(2,128)(2,1)}), bf16[2,16,12,768]{3,0,2,1:T(2,128)(2,1)}, u32[]{:S(2)}, u32[]{:S(2)}) async-start(bf16[2,16,12,768]{3,0,2,1:T(2,128)(2,1)} %bitcast.68), calls=%async_computation.5 | async-start | bytes 1179648 | tf_op jit(solution)/shard_map/all_to_all | solution.py:163
  537.4 15.2 %all-to-all-start.11 = ((bf16[2,16,12,768]{3,0,2,1:T(2,128)(2,1)}), bf16[2,16,12,768]{3,0,2,1:T(2,128)(2,1)}, u32[]{:S(2)}, u32[]{:S(2)}) async-start(bf16[2,16,12,768]{3,0,2,1:T(2,128)(2,1)} %bitcast.616), calls=%async_computation.11 | async-start | bytes 1179648 | tf_op jit(solution)/shard_map/all_to_all | solution.py:236
  542.1 65.1 %all-reduce.25.cloned.1.call-start = ((), (), s32[]{:S(2)}) async-start(), calls=%async_computation.21 | async-start | bytes 1179648 | tf_op jit(solution)/shard_map/psum | solution.py:244
  569.2 40.0 %copy-start.177 = (f32[128,2]{0,1:T(2,128)S(1)}, f32[128,2]{0,1:T(2,128)}, u32[]{:S(2)}) copy-start(f32[128,2]{0,1:T(2,128)} %copy-done.176) | copy-start | bytes 3076
  569.2 40.0 %copy-start.181 = (s32[128,2]{0,1:T(2,128)S(1)}, s32[128,2]{0,1:T(2,128)}, u32[]{:S(2)}) copy-start(s32[128,2]{0,1:T(2,128)} %get-tuple-element.129) | copy-start | bytes 3076
  569.2 40.1 %copy-start.185 = (s32[128,2]{0,1:T(2,128)S(1)}, s32[128,2]{0,1:T(2,128)}, u32[]{:S(2)}) copy-start(s32[128,2]{0,1:T(2,128)} %copy-done.183) | copy-start | bytes 3076
  569.2 40.1 %copy-start.6 = (bf16[128,768]{1,0:T(8,128)(2,1)S(1)}, bf16[128,768]{1,0:T(8,128)(2,1)}, u32[]{:S(2)}) copy-start(bf16[128,768]{1,0:T(8,128)(2,1)} %copy-done.5) | copy-start | bytes 589828
  569.2 40.1 %copy-start.17 = (bf16[2,128,768]{2,1,0:T(8,128)(2,1)S(1)}, bf16[2,128,768]{2,1,0:T(8,128)(2,1)}, u32[]{:S(2)}) copy-start(bf16[2,128,768]{2,1,0:T(8,128)(2,1)} %param.11) | copy-start | bytes 1179652
  569.2 40.1 %copy-start.26 = (f32[128,768]{1,0:T(8,128)S(1)}, f32[128,768]{1,0:T(8,128)}, u32[]{:S(2)}) copy-start(f32[128,768]{1,0:T(8,128)} %all-reduce.13.cloned.1.call-done) | copy-start | bytes 1179652
  569.2 40.1 %copy-start.91 = (bf16[1,768,32]{1,2,0:T(8,128)(2,1)S(1)}, bf16[1,768,32]{1,2,0:T(8,128)(2,1)}, u32[]{:S(2)}) copy-start(bf16[1,768,32]{1,2,0:T(8,128)(2,1)} %param.19) | copy-start | bytes 147460
  569.3 40.1 %copy-start.131 = (f32[768]{0:T(1024)S(1)}, f32[768]{0:T(1024)}, u32[]{:S(2)}) copy-start(f32[768]{0:T(1024)} %copy-done.128) | copy-start | bytes 9220
  569.3 40.1 %copy-start.212 = (f32[128]{0:T(128)S(1)}, f32[128]{0:T(128)}, u32[]{:S(2)}) copy-start(f32[128]{0:T(128)} %get-tuple-element.141) | copy-start | bytes 1540
  641.7 4.0 collective-permute-start.3
  656.5 24.1 %all-to-all-start.12 = ((bf16[32,1,12,768]{3,2,1,0:T(8,128)(2,1)}), bf16[32,1,12,768]{3,2,1,0:T(8,128)(2,1)}, u32[]{:S(2)}, u32[]{:S(2)}) async-start(bf16[32,1,12,768]{3,2,1,0:T(8,128)(2,1)} %bitcast.601), calls=%async_computation.12 | async-start | bytes 1572864 | tf_op jit(solution)/shard_map/all_to_all | solution.py:222
  688.3 17.0 %all-to-all-start.14 = ((bf16[2,16,12,768]{3,0,2,1:T(2,128)(2,1)}), bf16[2,16,12,768]{3,0,2,1:T(2,128)(2,1)}, u32[]{:S(2)}, u32[]{:S(2)}) async-start(bf16[2,16,12,768]{3,0,2,1:T(2,128)(2,1)} %bitcast.618), calls=%async_computation.14 | async-start | bytes 1179648 | tf_op jit(solution)/shard_map/all_to_all | solution.py:236
  692.5 59.8 %all-reduce.21.cloned.1.call-start = ((), (), s32[]{:S(2)}) async-start(), calls=%async_computation.19 | async-start | bytes 393216 | tf_op jit(solution)/shard_map/psum | solution.py:244
  714.9 37.5 %copy-start.4 = (bf16[128,768]{1,0:T(8,128)(2,1)S(1)}, bf16[128,768]{1,0:T(8,128)(2,1)}, u32[]{:S(2)}) copy-start(bf16[128,768]{1,0:T(8,128)(2,1)} %copy-done.1) | copy-start | bytes 589828
  714.9 37.5 %copy-start.7 = (bf16[128,768]{1,0:T(8,128)(2,1)S(1)}, bf16[128,768]{1,0:T(8,128)(2,1)}, u32[]{:S(2)}) copy-start(bf16[128,768]{1,0:T(8,128)(2,1)} %copy-done.5) | copy-start | bytes 589828
  714.9 37.5 %copy-start.28 = (f32[128,768]{1,0:T(8,128)S(1)}, f32[128,768]{1,0:T(8,128)}, u32[]{:S(2)}) copy-start(f32[128,768]{1,0:T(8,128)} %all-reduce.17.cloned.1.call-done) | copy-start | bytes 1179652
  714.9 37.5 %copy-start.30 = (f32[128,768]{1,0:T(8,128)S(1)}, f32[128,768]{1,0:T(8,128)}, u32[]{:S(2)}) copy-start(f32[128,768]{1,0:T(8,128)} %all-reduce.19.cloned.1.call-done) | copy-start | bytes 1179652
  714.9 150.3 %all-reduce.23.cloned.1.call-start = ((), (), s32[]{:S(2)}) async-start(), calls=%async_computation.20 | async-start | bytes 2359296 | tf_op jit(solution)/shard_map/psum | solution.py:342
  776.2 87.1 %copy-start.70 = (f32[128,768]{1,0:T(8,128)S(1)}, f32[128,768]{1,0:T(8,128)}, u32[]{:S(2)}) copy-start(f32[128,768]{1,0:T(8,128)} %copy-done.69) | copy-start | bytes 1179652
  (197 other events, 1025.7 us)
Sparse Core Ops, SparseCore 0:
  16.6 44.6 all-reduce.12
  113.3 39.0 all-reduce.14
  161.9 42.7 all-reduce.16
  310.3 43.6 all-reduce.26
  391.7 41.8 all-reduce.18
  564.5 42.7 all-reduce.24
  715.0 37.3 all-reduce.20
  774.8 86.9 all-reduce.22
